TPU v7x, 256 devices: a whole 4x4x8 slice. The times are simulated.
256 devices in a mesh: cont: 8 (over y, core), dev: 32 (over x, z).
Axes of the slice: x: 4, y: 4, z: 8, core: 2. Of those that a mesh axis runs over, the one named last changes fastest.
Arguments:
- station_values: bfloat16 [256, 128, 366], P(('cont', 'dev')), may hold values from -6 to 6
- krige_weights: bfloat16 [256, 128, 512], P(('cont', 'dev')), may hold values from -0.25 to 0.25
- inv_factor: bfloat16 [256, 128, 128], P(('cont', 'dev')), may hold values from -4 to 4
- cond_blocks: int32 [256, 4], P(('cont', 'dev')), may hold values from 0 to 255, as said below
- station_xy: bfloat16 [256, 2, 128], P(('cont', 'dev')), may hold values from 0 to 2
- cell_xy: float32 [2, 1048576], P(None, ('cont', 'dev')), may hold values from 0 to 2
- tile_blocks: int32 [1024, 16], P(('cont', 'dev')), may hold values from 0 to 255, as said below
- rain: float32 [60, 1048576], P(None, ('cont', 'dev')), may hold values from -6 to 6
Outputs:
- thresholds: bfloat16 [1048576, 366], P(('cont', 'dev'))
- exceed_share: float32 [1048576], P(('cont', 'dev'))
Inputs may be any that keep to these rules, and one draw needn't show every extreme that they name: `cond_blocks`: row b names 4 different blocks of b's continent c (blocks c * 32 to c * 32 + 31), never b itself. `tile_blocks`: row t names 16 different blocks, each of the continent of tile t or of the continent before it (continent c - 1, and 7 before 0); tile t lies in continent t // 128.
All inputs are finite; a program needn't handle non-finite values.
Results may differ from a plain program's by a relative error of at most 0.0069.
Values may be sent and summed in bfloat16 or wider, within the bound.
A program may use at most 64 MiB of HBM per device.

v0:
```python
import heapq
import math

import jax
import jax.numpy as jnp
from jax import lax
from jax.experimental import pallas as pl
from jax.experimental.pallas import tpu as pltpu
from jax.sharding import PartitionSpec as P

MESH = pl.DeviceIdType.MESH
BF16 = jnp.bfloat16
F32 = jnp.float32

XS, ZS = 4, 8
GROUP = XS * ZS
CONTS = 8
BS = 128
DAYS = 366
ROWS = 368
SV_A, KW_A = 176, 192
NCOND = 4
LISTED = 16
STATIONS = LISTED * BS
TILES = 4
TILE = 1024
CELLS = TILES * TILE
WIN = 60
WSTART = 150
WROW = WSTART // 8 * 8
WOFF = WSTART - WROW
WROWS = -(-(WOFF + WIN) // 8) * 8
LENGTH = 9.0 * STATIONS**-0.5
SCALE = math.log2(math.e) / LENGTH
NUGGET = (LENGTH * 0.1 * SCALE) ** 2


class Place:
    def __init__(self):
        self.dev, self.cont = lax.axis_index("dev"), lax.axis_index("cont")
        self.x, self.z = self.dev // ZS, self.dev % ZS
        self.xs = {s: lax.rem(self.x + (s + XS), XS) for s in (-1, 0, 1, 2)}
        self.zs = {s: lax.rem(self.z + (s + ZS), ZS) for s in (-3, -2, -1, 0, 1, 2, 3, 4)}
        self.ahead = lax.rem(self.cont + 1, CONTS)
        self.behind = lax.rem(self.cont + CONTS - 1, CONTS)
        self.even = lax.rem(self.cont, 2) == 0

    def toward(self, way):
        axis, step = way
        if axis == "cont":
            return {"cont": self.ahead}
        x, z = (self.xs[step], self.z) if axis == "x" else (self.x, self.zs[step])
        return {"dev": x * ZS + z}


def remote(src, dst, send, recv, device):
    return pltpu.make_async_remote_copy(
        src_ref=src, dst_ref=dst, send_sem=send, recv_sem=recv, device_id=device, device_id_type=MESH
    )


def along_x_first(item):
    dx, dz, part = item
    sends = []
    if dz == 0:
        if dx == 0:
            sends += [(("x", s), (-s, 0, 0)) for s in (1, -1)] + [(("x", 2), (2, 0, 0))]
        sends += [(("z", s), (dx, -s, 0)) for s in (1, -1)]
    elif abs(dz) < 3 or (abs(dz) == 3 and (dz < 0) == (dx in (0, 1))):
        step = 1 if dz < 0 else -1
        far = dz - step
        sends.append((("z", step), (dx, 4 if abs(far) == 4 else far, 0)))
    return sends


def along_z_first(item):
    dx, dz, part = item
    sends = []
    if dx == 0:
        if dz == 0:
            sends += [(("z", s), (0, -s, 0)) for s in (1, -1)]
        elif abs(dz) < 3:
            step = 1 if dz < 0 else -1
            sends.append((("z", step), (0, dz - step, 0)))
        elif abs(dz) == 3:
            step = 1 if dz < 0 else -1
            sends.append((("z", step), (0, 4, step)))
        sends += [(("x", s), (-s, dz, 0)) for s in (1, -1)]
        if dz == 4:
            sends.append((("x", 2), (2, 4, 0)))
    elif dx != 2 and dz != 4:
        if dz == 0:
            sends.append((("x", -dx), (2, 0, dx)))
        elif (dz < 0) == (dx < 0):
            sends.append((("x", -dx), (2, dz, 0)))
    return sends


def items_of(sends_of):
    found, todo = [], [(0, 0, 0)]
    while todo:
        item = todo.pop(0)
        found.append(item)
        if item[2] == 0:
            todo += [arrival for _, arrival in sends_of(item)]
        elif (*item[:2], 0) not in found:
            todo.append((*item[:2], 0))
            found.append((*item[:2], 0))
            todo.pop()
            todo += [arrival for _, arrival in sends_of((*item[:2], 0))]
    return list(dict.fromkeys(found))


SENDS = {"a": along_x_first, "b": along_z_first}
ITEMS = {kind: items_of(sends) for kind, sends in SENDS.items()}
SEM = {kind: {item: i for i, item in enumerate(items)} for kind, items in ITEMS.items()}
HALF_ROWS = {"sv": {"a": SV_A, "b": ROWS - SV_A}, "kw": {"a": KW_A, "b": ROWS - KW_A}}


class Gather:
    def __init__(self, place, kind, buf, send, recv):
        self.place, self.kind, self.buf, self.send, self.recv = place, kind, buf, send, recv
        self.rows = buf.shape[1]

    def ref(self, item):
        dx, dz, part = item
        x, z = self.place.xs[dx], self.place.zs[dz]
        slot = z * XS + x if self.kind == "a" else x * ZS + z
        if part == 0:
            return self.buf.at[slot]
        cut = self.rows // 32 * 16
        first, last = (0, cut) if part < 0 else (cut, self.rows)
        return self.buf.at[slot, pl.ds(first, last - first)]

    def send_on(self, item, index):
        way, arrival = SENDS[self.kind](item)[index]
        ref = self.ref((*item[:2], arrival[2]))
        sem = self.recv.at[SEM[self.kind][arrival]]
        remote(ref, ref, self.send, sem, self.place.toward(way)).start()

    def arrive(self, item):
        ref = self.ref(item)
        sem = self.recv.at[SEM[self.kind][item]]
        remote(ref, ref, self.send, sem, {"dev": self.place.dev}).wait_recv()

    def sent(self):
        ref = self.buf.at[pl.ds(0, GROUP - 1)]
        remote(ref, ref, self.send, self.recv.at[0], {"dev": self.place.dev}).wait_send()


RATE, HOP, MORE, CORE_RATE, CORE_HOP, ISSUE = 92e3, 3.2, 0.62, 1.4e6, 0.75, 0.08
KRIGING = 0.8
STEP_COST = 0.28
READY = 14.0


LEND = {"a": XS, "b": ZS}
DEPTH = 1.0


def chain(kind, item):
    return max([1 + chain(kind, (*to[:2], 0)) for _, to in SENDS[kind](item)], default=0)


def schedule():
    links, queue, clock = {}, [], [0.0, 0.0]
    plan, whole, got, lent, count = [], {}, {}, {}, 0
    left = [TILES * LISTED] * 2
    waiting = ([], [])

    def post(core, way, size, target, arrival):
        nonlocal count
        clock[core] += ISSUE
        end = clock[core]
        if way == ("cont", 0):
            end += size / CORE_RATE + CORE_HOP
        else:
            lanes = [(way[0], 1), (way[0], -1)] if way[1] == 2 else [way]
            for lane in lanes:
                links[lane] = max(clock[core], links.get(lane, 0.0)) + size / RATE
                end = max(end, links[lane])
            end += HOP + (MORE if way[1] == 2 else 0.0)
        count += 1
        heapq.heappush(queue, (end, count, target, arrival))

    def flush(core):
        later = []
        soon = queue[0][0] if queue else 1e9
        for entry in sorted(waiting[core]):
            _, _, index, stage, kind, source, item = entry
            way, arrival = SENDS[kind](item)[index]
            lanes = [(way[0], 1), (way[0], -1)] if way[1] == 2 else [way]
            free = min(links.get(lane, 0.0) for lane in lanes)
            if free > max(clock[core] + DEPTH, soon):
                later.append(entry)
                continue
            size = HALF_ROWS[stage][kind] * BS * 2
            post(core, way, size if arrival[2] == 0 else size / 2, core, (stage, kind, source, arrival))
            if core == 0:
                plan.append(("send", stage, kind, source, item, clock[0], index))
        waiting[core][:] = later

    def forward(core, stage, kind, source, item):
        nonlocal count
        size = HALF_ROWS[stage][kind] * BS * 2
        if kind == "b" and core == 1 and stage == "kw" and item == (0, 0, 0):
            post(1, ("y", 1), size, 0, (stage, kind, "prev", item))
        if source == "own" or (kind == "b" and core == 0):
            for index, (way, arrival) in enumerate(SENDS[kind](item)):
                count += 1
                ahead = chain(kind, (*arrival[:2], 0))
                waiting[core].append((-ahead, count, index, stage, kind, source, item))
        if source == "own" and stage == "kw" and (kind == "a" or core == 0):
            group = item[1] if kind == "a" else item[0]
            size *= LEND[kind]
            have = lent[core, kind, group] = lent.get((core, kind, group), 0) + 1
            if have % LEND[kind]:
                return
            way = ("cont", 0) if core == 0 else ("y", 1)
            post(core, way, size, 1 - core, (stage, kind, "prev", item))
            if core == 0:
                plan.append(("lend", stage, kind, source, item, clock[0]))

    for kind in ("b", "a"):
        for core in (0, 1):
            forward(core, "sv", kind, "own", (0, 0, 0))
    while queue or waiting[0] or waiting[1]:
        for core in (0, 1):
            flush(core)
        if not queue:
            continue
        when, _, core, (stage, kind, source, item) = heapq.heappop(queue)
        passive = source == "prev" and (kind == "a" or core == 1)
        if passive:
            continue
        while left[core] and when - max(clock[core], READY) > STEP_COST / 4:
            clock[core] = max(clock[core], READY) + STEP_COST
            left[core] -= 1
            if core == 0 and plan[-1][0] == "cover":
                plan[-1] = ("cover", plan[-1][1] + 1)
            elif core == 0:
                plan.append(("cover", 1))
            flush(core)
        clock[core] = max(clock[core], when) + ISSUE
        if core == 0:
            plan.append(("arrive", stage, kind, source, item, clock[0]))
        if item[2]:
            item = (*item[:2], 0)
            key = (core, stage, kind, source, item)
            whole[key] = whole.get(key, 0) + 1
            if whole[key] < 2:
                continue
        forward(core, stage, kind, source, item)
        if stage == "sv":
            got[core, kind] = got.get((core, kind), 1) + 1
            ready = []
            if kind == "b" and got[core, "b"] == GROUP:
                ready.append("b")
            if got.get((core, "a")) == got.get((core, "b")) == GROUP:
                ready.append("a")
            for half in ready:
                clock[core] += KRIGING
                if core == 0:
                    plan.append(("krige", half))
                forward(core, "kw", half, "own", (0, 0, 0))
    plan.append(("cover", left[0]))
    return plan


def dot(a, b, dims=((1,), (0,))):
    return lax.dot_general(a, b, (dims, ((), ())), preferred_element_type=F32)


def kernel(
    cond_hbm, tiles_hbm, sv_hbm, weights_hbm, factor_hbm, xy_hbm, cells_hbm, rain,
    out, share,
    cond, tiles, sv, weights, factor, xy, cells, in_sem,
    sva, svb, kwa, kwb, row_coords, coords, cellx, celly, rain_raw, rain_win, prior, cov, chosen_a, chosen_b,
    rain_sem,
    c_send, c_recv, cz_send, cc_send,
    sa_send, sa_recv, sb_send, sb_recv,
    ka_send, ka_recv, kb_send, kb_recv, kp_send, kp_recv,
    fa_send, fa_recv, fb_send, fb_recv, inj_send, inj_recv,
):
    p = Place()
    odd = jnp.logical_not(p.even)
    slot_a, slot_b = p.z * XS + p.x, p.dev
    here = {"dev": p.dev}
    gathers = {
        ("sv", "a", "own"): Gather(p, "a", sva, sa_send, sa_recv),
        ("sv", "b", "own"): Gather(p, "b", svb, sb_send, sb_recv),
        ("kw", "a", "own"): Gather(p, "a", kwa.at[1], ka_send, ka_recv),
        ("kw", "b", "own"): Gather(p, "b", kwb.at[1], kb_send, kb_recv),
        ("kw", "b", "prev"): Gather(p, "b", kwb.at[0], kp_send, kp_recv),
    }
    barrier = pltpu.get_barrier_semaphore()
    x_ways = [("x", s) for s in (1, -1, 2)]
    z_ways = [("z", s) for s in (1, -1, 2, -2, 3, -3, 4)]
    for way in x_ways + z_ways:
        pl.semaphore_signal(barrier, inc=1, device_id=p.toward(way), device_id_type=MESH)
    pl.semaphore_signal(barrier, inc=1, device_id={"cont": p.behind}, device_id_type=MESH)

    arrays = (
        (sv_hbm, sv), (xy_hbm, xy), (cells_hbm, cells), (cond_hbm, cond), (tiles_hbm, tiles),
        (weights_hbm, weights), (factor_hbm, factor),
    )
    loads = [pltpu.make_async_copy(*pair, in_sem.at[i]) for i, pair in enumerate(arrays)]
    for load in loads:
        load.start()
    rain_copy = pltpu.make_async_copy(rain, rain_raw, rain_sem)
    rain_copy.start()
    loads[0].wait()
    loads[1].wait()
    sva[slot_a] = sv[0, :SV_A, :]
    svb[slot_b] = jnp.concatenate(
        [sv[0, SV_A:, :], jnp.zeros((ROWS - DAYS, BS), BF16)], axis=0
    )
    row_coords[p.x] = jnp.concatenate(
        [xy[0].astype(F32) * SCALE, jnp.zeros((6, BS), F32)], axis=0
    )
    pl.semaphore_wait(barrier, XS + ZS - 1)

    own = row_coords.at[p.x]
    for i, way in enumerate(x_ways):
        remote(own, own, c_send, c_recv.at[i], p.toward(way)).start()

    def coords_x():
        for i, (_, s) in enumerate(x_ways):
            ref = row_coords.at[p.xs[2 if s == 2 else -s]]
            remote(ref, ref, c_send, c_recv.at[i], here).wait_recv()
        coords[1, p.z] = jnp.concatenate([row_coords[x, 0:2, :] for x in range(XS)], axis=0)
        ref = coords.at[1, p.z]
        for i, way in enumerate(z_ways):
            remote(ref, ref, cz_send, c_recv.at[3 + i], p.toward(way)).start()

    coord_ahead = remote(coords.at[1], coords.at[0], cc_send, c_recv.at[10], {"cont": p.ahead})

    def coords_z():
        for i, (_, s) in enumerate(z_ways):
            ref = coords.at[1, p.zs[4 if s == 4 else -s]]
            remote(ref, ref, cz_send, c_recv.at[3 + i], here).wait_recv()
        coord_ahead.start()

    def place_cells(first, last):
        def one(c, carry):
            lanes = pl.ds(pl.multiple_of(c * 128, 128), 128)
            for row, held in ((0, cellx), (1, celly)):
                line = cells[row : row + 1, lanes] * SCALE
                held[lanes, :] = jnp.transpose(jnp.broadcast_to(line, (128, 128)))
            return carry

        lax.fori_loop(first, last, one, 0)

    def place_rain():
        rain_copy.wait()
        rain_win[...] = jnp.zeros_like(rain_win)
        rain_win[WOFF : WOFF + WIN, :] = rain_raw[...]

    def listed(t, k):
        block = tiles[t, k]
        own = jnp.where(block // GROUP == p.cont, 1, 0)
        dev = block % GROUP
        return own, dev % ZS * XS + dev // ZS, dev

    def cover(first, last):
        def one(g, carry):
            t, k = g // LISTED, g % LISTED
            own, _, dev = listed(t, k)
            x, z = dev // ZS, dev % ZS
            sx, sy = coords[own, z, pl.ds(2 * x, 1), :], coords[own, z, pl.ds(2 * x + 1, 1), :]
            lanes = pl.ds(pl.multiple_of(k * BS, BS), BS)

            def part(c, carry):
                rows = pl.ds(pl.multiple_of(t * TILE + c * 256, 256), 256)
                dx = cellx[rows, :] - sx
                dy = celly[rows, :] - sy
                square = dx * dx + dy * dy + NUGGET
                cov[rows, lanes] = jnp.exp2(-4.0 - square * lax.rsqrt(square)).astype(BF16)
                return carry

            return lax.fori_loop(0, TILE // 256, part, carry)

        lax.fori_loop(first, last, one, 0)

    def krige(kind):
        first, last = (0, KW_A) if kind == "a" else (KW_A, ROWS)

        def days(dev):
            below = sva[dev % ZS * XS + dev // ZS, first:SV_A, :] if first < SV_A else None
            above = svb[dev, max(first - SV_A, 0) : last - SV_A, :]
            return above if below is None else jnp.concatenate([below, above], axis=0)

        rows = pl.ds(first, last - first)
        for k in range(NCOND):
            prior[rows, k * BS : (k + 1) * BS] = days(cond[0, k] % GROUP)
        predicted = dot(prior[rows, :], weights[0], ((1,), (1,)))
        innovation = (days(p.dev).astype(F32) - predicted).astype(BF16)
        whitened = dot(innovation, factor[0], ((1,), (1,))).astype(BF16)
        kweights = dot(whitened, factor[0]).astype(BF16)
        if kind == "a":
            kwa[1, slot_a] = kweights
        else:
            kwb[1, slot_b] = kweights

            @pl.when(odd)
            def _():
                remote(
                    kwb.at[1, slot_b], kwb.at[0, slot_b], inj_send, inj_recv, {"cont": p.ahead}
                ).start()

    def lend(kind, item):
        buf, send, recv = (kwa, fa_send, fa_recv) if kind == "a" else (kwb, fb_send, fb_recv)
        x, z = p.xs[item[0]], p.zs[item[1]]
        part = pl.ds(z * XS, XS) if kind == "a" else pl.ds(x * ZS, ZS)
        remote(buf.at[1, part], buf.at[0, part], send, recv, {"cont": p.ahead}).start()

    def act(step):
        what, stage, kind, source, item = step[:5]
        if what == "send":
            gathers[stage, kind, source].send_on(item, step[6])
        elif what == "lend" and kind == "a":
            lend(kind, item)
        elif what == "lend":
            pl.when(p.even)(lambda: lend(kind, item))
        elif source == "prev" and item == (0, 0, 0):
            ref = kwb.at[0, slot_b]
            remote(ref, ref, inj_send, inj_recv, here).wait_recv()
        else:
            gathers[stage, kind, source].arrive(item)

    def finish_loads():
        for load in loads[2:]:
            load.wait()

    early = [
        (1.0, finish_loads),
        (1.0, lambda: place_cells(0, 8)),
        (3.4, coords_x),
        (4.0, lambda: place_cells(8, 16)),
        (7.0, lambda: place_cells(16, 24)),
        (9.0, coords_z),
        (9.0, lambda: place_cells(24, CELLS // 128)),
        (READY - 1.0, place_rain),
        (READY - 1.0, coord_ahead.wait_recv),
    ]
    done = 0
    steps = schedule()
    while steps:
        step = steps.pop(0)
        if step[0] == "cover":
            cover(done, done + step[1])
            done += step[1]
        elif step[0] == "krige":
            krige(step[1])
        else:
            while early and early[0][0] < step[5]:
                early.pop(0)[1]()
            batch = [step]
            if step[3] == "prev":
                while steps and len(steps[0]) > 2 and steps[0][3] == "prev":
                    batch.append(steps.pop(0))

                @pl.when(p.even)
                def _(batch=batch):
                    for one in batch:
                        act(one)
            else:
                act(step)

    whole = kwa.at[0]
    remote(whole, whole, fa_send, fa_recv, here).wait_recv()

    @pl.when(odd)
    def _():
        ref = kwb.at[0]
        remote(ref, ref, fb_send, fb_recv, here).wait_recv()

    def choose(t, chosen):
        for k in range(LISTED):
            own, at, dev = listed(t, k)
            chosen[:KW_A, k * BS : (k + 1) * BS] = kwa[own, at]
            chosen[KW_A:, k * BS : (k + 1) * BS] = kwb[own, dev]

    def tile(t, chosen):
        at = pl.ds(pl.multiple_of(t * TILE, TILE), TILE)
        full = dot(chosen[...], cov[at, :], ((1,), (1,)))
        out[:, at] = full[:DAYS].astype(BF16)
        soft = jnp.tanh((rain_win[:, at] - full[WROW : WROW + WROWS]) * 2.0)
        row = lax.broadcasted_iota(jnp.int32, soft.shape, 0)
        soft = jnp.where((row >= WOFF) & (row < WOFF + WIN), soft, 0.0)
        total = jnp.sum(soft, axis=0, keepdims=True)
        share[:, at] = total * (0.5 / WIN) + 0.5

    def two_tiles(i, carry):
        choose(2 * i + 1, chosen_b)
        tile(2 * i, chosen_a)
        choose(jnp.minimum(2 * i + 2, TILES - 1), chosen_a)
        tile(2 * i + 1, chosen_b)
        return carry

    choose(0, chosen_a)
    lax.fori_loop(0, TILES // 2, two_tiles, 0)

    for (_, _, source), gather in gathers.items():
        if source == "own":
            gather.sent()
    ref = row_coords.at[pl.ds(0, XS - 1)]
    remote(ref, ref, c_send, c_recv.at[0], here).wait_send()
    ref = coords.at[1, pl.ds(0, ZS - 1)]
    remote(ref, ref, cz_send, c_recv.at[0], here).wait_send()
    coord_ahead.wait_send()
    remote(whole, whole, fa_send, fa_recv, here).wait_send()

    @pl.when(odd)
    def _():
        remote(
            kwb.at[1, slot_b], kwb.at[0, slot_b], inj_send, inj_recv, {"cont": p.ahead}
        ).wait_send()

    @pl.when(p.even)
    def _():
        gathers["kw", "b", "prev"].sent()
        ref = kwb.at[1]
        remote(ref, ref, fb_send, fb_recv, here).wait_send()


def per_device(sv, weights, factor, cond, xy, cells, tiles, rain):
    dma = pltpu.SemaphoreType.DMA
    vmem, hbm = pl.BlockSpec(memory_space=pltpu.VMEM), pl.BlockSpec(memory_space=pltpu.HBM)
    inputs = (cond, tiles, jnp.swapaxes(sv, 1, 2), weights, factor, xy, cells, rain)
    inputs = [pltpu.with_memory_space_constraint(a, pltpu.HBM) for a in inputs]
    thresholds, share = pl.pallas_call(
        kernel,
        out_shape=(
            jax.ShapeDtypeStruct((DAYS, CELLS), BF16),
            jax.ShapeDtypeStruct((1, CELLS), F32),
        ),
        in_specs=[hbm] * len(inputs),
        out_specs=(vmem, vmem),
        scratch_shapes=[
            pltpu.SMEM(cond.shape, jnp.int32),
            pltpu.SMEM(tiles.shape, jnp.int32),
            *(pltpu.VMEM(a.shape, a.dtype) for a in inputs[2:7]),
            dma((7,)),
            pltpu.VMEM((GROUP, SV_A, BS), BF16),
            pltpu.VMEM((GROUP, ROWS - SV_A, BS), BF16),
            pltpu.VMEM((2, GROUP, KW_A, BS), BF16),
            pltpu.VMEM((2, GROUP, ROWS - KW_A, BS), BF16),
            pltpu.VMEM((XS, 8, BS), F32),
            pltpu.VMEM((2, ZS, 2 * XS, BS), F32),
            pltpu.VMEM((CELLS, 128), F32),
            pltpu.VMEM((CELLS, 128), F32),
            pltpu.VMEM((WIN, CELLS), F32),
            pltpu.VMEM((WROWS, CELLS), F32),
            pltpu.VMEM((ROWS, NCOND * BS), BF16),
            pltpu.VMEM((CELLS, STATIONS), BF16),
            pltpu.VMEM((ROWS, STATIONS), BF16),
            pltpu.VMEM((ROWS, STATIONS), BF16),
            dma,
            dma, dma((XS + ZS - 1,)), dma, dma,
            dma, dma((len(ITEMS["a"]),)), dma, dma((len(ITEMS["b"]),)),
            dma, dma((len(ITEMS["a"]),)), dma, dma((len(ITEMS["b"]),)), dma, dma((len(ITEMS["b"]),)),
            dma, dma, dma, dma, dma, dma,
        ],
        compiler_params=pltpu.CompilerParams(
            collective_id=0, has_side_effects=True, vmem_limit_bytes=44 * 1024 * 1024
        ),
    )(*inputs)
    return thresholds.T, share.reshape(-1)


def solution(mesh):
    both = ("cont", "dev")
    placed = (
        P(both, None, None),
        P(both, None, None),
        P(both, None, None),
        P(both, None),
        P(both, None, None),
        P(None, both),
        P(both, None),
        P(None, both),
    )
    return jax.shard_map(
        per_device,
        mesh=mesh,
        in_specs=placed,
        out_specs=(P(both, None), P(both)),
        check_vma=False,
    )
```

profile of v0, /device:TPU:1, one launch (start us, length us, event | category | flops | bytes accessed | tf_op | source)
XLA Modules:
  0.0 73.4 jit_solution(4076252260284575212)
XLA Ops:
  0.6 70.5 %shard_map.95 = (bf16[366,4096]{1,0:T(8,128)(2,1)S(1)}, f32[1,4096]{1,0:T(1,128)S(1)}) custom-call(s32[1,4]{1,0:T(1,128)} %cond_hbm.1, s32[4,16]{1,0:T(4,128)} %tiles_hbm.1, bf16[1,366,128]{2,1,0:T(8,128)(2,1)} %bitcast.5, bf16[1,128,512]{2,1,0:T(8,128)(2,1)} %weights_hbm.1, bf16[1,128,128]{2,1,0:T(8,128)(2,1)} %factor_hbm.1, bf16[1,2,128]{2,1,0:T(2,128)(2,1)} %xy_hbm.1, ...), custom_call_target="tpu_custom_call" | custom-call | tf_op jit(solution)/shard_map/pallas_call | solution.py:532
  71.2 1.6 %copy.12 = bf16[4096,366]{0,1:T(8,128)(2,1)} copy(bf16[4096,366]{0,1:T(8,128)(2,1)S(1)} %bitcast.3) | data formatting | bytes 5996544
  72.8 0.6 copy.13
where the time goes:
time: 73.5 us; the launch traced here: 73.4 us
  Pallas kernels  70.5 us (96%)
  local copies, waits for them, and re-layouts  2.23 us (3%)
    pallas_call x1, Pallas kernels, per_device(): pl.pallas_call(kernel, out_shape=(jax.ShapeDtypeStruct((DAYS, CELLS), BF1...  70.5 us
    unnamed x2, local copies, waits for them, and re-layouts  2.23 us

commit v1 on v0

--- a/solution.py
+++ b/solution.py
@@ -271,11 +271,18 @@
     return lax.dot_general(a, b, (dims, ((), ())), preferred_element_type=F32)
 
 
+def listing(tiles, cont, t, k):
+    block = tiles[t, k]
+    own = jnp.where(block // GROUP == cont, 1, 0)
+    dev = block % GROUP
+    return own, dev % ZS * XS + dev // ZS, dev
+
+
 def kernel(
     cond_hbm, tiles_hbm, sv_hbm, weights_hbm, factor_hbm, xy_hbm, cells_hbm, rain,
-    out, share,
+    kwa, kwb, cov, rain_win, tiles_kept,
     cond, tiles, sv, weights, factor, xy, cells, in_sem,
-    sva, svb, kwa, kwb, row_coords, coords, cellx, celly, rain_raw, rain_win, prior, cov, chosen_a, chosen_b,
+    sva, svb, row_coords, coords, cellx, celly, rain_raw, prior,
     rain_sem,
     c_send, c_recv, cz_send, cc_send,
     sa_send, sa_recv, sb_send, sb_recv,
@@ -302,7 +309,7 @@
 
     arrays = (
         (sv_hbm, sv), (xy_hbm, xy), (cells_hbm, cells), (cond_hbm, cond), (tiles_hbm, tiles),
-        (weights_hbm, weights), (factor_hbm, factor),
+        (weights_hbm, weights), (factor_hbm, factor), (tiles_hbm, tiles_kept),
     )
     loads = [pltpu.make_async_copy(*pair, in_sem.at[i]) for i, pair in enumerate(arrays)]
     for load in loads:
@@ -357,10 +364,7 @@
         rain_win[WOFF : WOFF + WIN, :] = rain_raw[...]
 
     def listed(t, k):
-        block = tiles[t, k]
-        own = jnp.where(block // GROUP == p.cont, 1, 0)
-        dev = block % GROUP
-        return own, dev % ZS * XS + dev // ZS, dev
+        return listing(tiles, p.cont, t, k)
 
     def cover(first, last):
         def one(g, carry):
@@ -475,32 +479,6 @@
         ref = kwb.at[0]
         remote(ref, ref, fb_send, fb_recv, here).wait_recv()
 
-    def choose(t, chosen):
-        for k in range(LISTED):
-            own, at, dev = listed(t, k)
-            chosen[:KW_A, k * BS : (k + 1) * BS] = kwa[own, at]
-            chosen[KW_A:, k * BS : (k + 1) * BS] = kwb[own, dev]
-
-    def tile(t, chosen):
-        at = pl.ds(pl.multiple_of(t * TILE, TILE), TILE)
-        full = dot(chosen[...], cov[at, :], ((1,), (1,)))
-        out[:, at] = full[:DAYS].astype(BF16)
-        soft = jnp.tanh((rain_win[:, at] - full[WROW : WROW + WROWS]) * 2.0)
-        row = lax.broadcasted_iota(jnp.int32, soft.shape, 0)
-        soft = jnp.where((row >= WOFF) & (row < WOFF + WIN), soft, 0.0)
-        total = jnp.sum(soft, axis=0, keepdims=True)
-        share[:, at] = total * (0.5 / WIN) + 0.5
-
-    def two_tiles(i, carry):
-        choose(2 * i + 1, chosen_b)
-        tile(2 * i, chosen_a)
-        choose(jnp.minimum(2 * i + 2, TILES - 1), chosen_a)
-        tile(2 * i + 1, chosen_b)
-        return carry
-
-    choose(0, chosen_a)
-    lax.fori_loop(0, TILES // 2, two_tiles, 0)
-
     for (_, _, source), gather in gathers.items():
         if source == "own":
             gather.sent()
@@ -524,38 +502,81 @@
         remote(ref, ref, fb_send, fb_recv, here).wait_send()
 
 
+def interpolate(
+    kwa, kwb, cov, rain_win, tiles_kept, out, share, chosen_a, chosen_b, stage, out_sem, tiles, sem
+):
+    load = pltpu.make_async_copy(tiles_kept, tiles, sem)
+    load.start()
+    load.wait()
+    cont = lax.axis_index("cont")
+
+    def listed(t, k):
+        return listing(tiles, cont, t, k)
+
+    def choose(t, chosen):
+        for k in range(LISTED):
+            own, at, dev = listed(t, k)
+            chosen[:KW_A, k * BS : (k + 1) * BS] = kwa[own, at]
+            chosen[KW_A:, k * BS : (k + 1) * BS] = kwb[own, dev]
+
+    def copy_out(t, slot):
+        at = pl.ds(pl.multiple_of(t * TILE, TILE), TILE)
+        return pltpu.make_async_copy(stage.at[slot], out.at[:, at], out_sem.at[slot])
+
+    def tile(t, chosen, slot):
+        at = pl.ds(pl.multiple_of(t * TILE, TILE), TILE)
+        full = dot(chosen[...], cov[at, :], ((1,), (1,)))
+        held = stage.at[slot]
+        held[...] = full[:DAYS].astype(BF16)
+        copy_out(t, slot).start()
+        soft = jnp.tanh((rain_win[:, at] - full[WROW : WROW + WROWS]) * 2.0)
+        row = lax.broadcasted_iota(jnp.int32, soft.shape, 0)
+        soft = jnp.where((row >= WOFF) & (row < WOFF + WIN), soft, 0.0)
+        total = jnp.sum(soft, axis=0, keepdims=True)
+        share[at] = (total * (0.5 / WIN) + 0.5)[0]
+
+    def two_tiles(i, carry):
+        choose(2 * i + 1, chosen_b)
+        tile(2 * i, chosen_a, 2 * i)
+        choose(jnp.minimum(2 * i + 2, TILES - 1), chosen_a)
+        tile(2 * i + 1, chosen_b, 2 * i + 1)
+        return carry
+
+    choose(0, chosen_a)
+    lax.fori_loop(0, TILES // 2, two_tiles, 0)
+    for t in range(TILES):
+        copy_out(t, t).wait()
+
+
 def per_device(sv, weights, factor, cond, xy, cells, tiles, rain):
     dma = pltpu.SemaphoreType.DMA
     vmem, hbm = pl.BlockSpec(memory_space=pltpu.VMEM), pl.BlockSpec(memory_space=pltpu.HBM)
     inputs = (cond, tiles, jnp.swapaxes(sv, 1, 2), weights, factor, xy, cells, rain)
     inputs = [pltpu.with_memory_space_constraint(a, pltpu.HBM) for a in inputs]
-    thresholds, share = pl.pallas_call(
+    found = pl.pallas_call(
         kernel,
         out_shape=(
-            jax.ShapeDtypeStruct((DAYS, CELLS), BF16),
-            jax.ShapeDtypeStruct((1, CELLS), F32),
+            jax.ShapeDtypeStruct((2, GROUP, KW_A, BS), BF16),
+            jax.ShapeDtypeStruct((2, GROUP, ROWS - KW_A, BS), BF16),
+            jax.ShapeDtypeStruct((CELLS, STATIONS), BF16),
+            jax.ShapeDtypeStruct((WROWS, CELLS), F32),
+            jax.ShapeDtypeStruct(tiles.shape, jnp.int32),
         ),
         in_specs=[hbm] * len(inputs),
-        out_specs=(vmem, vmem),
+        out_specs=(vmem,) * 5,
         scratch_shapes=[
             pltpu.SMEM(cond.shape, jnp.int32),
             pltpu.SMEM(tiles.shape, jnp.int32),
             *(pltpu.VMEM(a.shape, a.dtype) for a in inputs[2:7]),
-            dma((7,)),
+            dma((8,)),
             pltpu.VMEM((GROUP, SV_A, BS), BF16),
             pltpu.VMEM((GROUP, ROWS - SV_A, BS), BF16),
-            pltpu.VMEM((2, GROUP, KW_A, BS), BF16),
-            pltpu.VMEM((2, GROUP, ROWS - KW_A, BS), BF16),
             pltpu.VMEM((XS, 8, BS), F32),
             pltpu.VMEM((2, ZS, 2 * XS, BS), F32),
             pltpu.VMEM((CELLS, 128), F32),
             pltpu.VMEM((CELLS, 128), F32),
             pltpu.VMEM((WIN, CELLS), F32),
-            pltpu.VMEM((WROWS, CELLS), F32),
             pltpu.VMEM((ROWS, NCOND * BS), BF16),
-            pltpu.VMEM((CELLS, STATIONS), BF16),
-            pltpu.VMEM((ROWS, STATIONS), BF16),
-            pltpu.VMEM((ROWS, STATIONS), BF16),
             dma,
             dma, dma((XS + ZS - 1,)), dma, dma,
             dma, dma((len(ITEMS["a"]),)), dma, dma((len(ITEMS["b"]),)),
@@ -563,10 +584,29 @@
             dma, dma, dma, dma, dma, dma,
         ],
         compiler_params=pltpu.CompilerParams(
-            collective_id=0, has_side_effects=True, vmem_limit_bytes=44 * 1024 * 1024
+            collective_id=0, has_side_effects=True, vmem_limit_bytes=14 * 1024 * 1024
         ),
     )(*inputs)
-    return thresholds.T, share.reshape(-1)
+    found = [pltpu.with_memory_space_constraint(a, pltpu.VMEM) for a in found]
+    thresholds, share = pl.pallas_call(
+        interpolate,
+        out_shape=(
+            jax.ShapeDtypeStruct((DAYS, CELLS), BF16),
+            jax.ShapeDtypeStruct((CELLS,), F32),
+        ),
+        in_specs=[vmem] * len(found),
+        out_specs=(hbm, vmem),
+        scratch_shapes=[
+            pltpu.VMEM((ROWS, STATIONS), BF16),
+            pltpu.VMEM((ROWS, STATIONS), BF16),
+            pltpu.VMEM((TILES, DAYS, TILE), BF16),
+            dma((TILES,)),
+            pltpu.SMEM(tiles.shape, jnp.int32),
+            dma,
+        ],
+        compiler_params=pltpu.CompilerParams(vmem_limit_bytes=16 * 1024 * 1024),
+    )(*found)
+    return thresholds.T, share
 
 
 def solution(mesh):

time: 73.5 us -> 73.4 us (level)
  local copies, waits for them, and re-layouts: 2.23 us -> 0 us
  Pallas kernels: 70.5 us -> 72.6 us
    unnamed x2 -> x0, local copies, waits for them, and re-layouts: 2.23 us -> none
    pallas_call x1 -> x2, Pallas kernels: 70.5 us -> 72.6 us  [the longest x1 63.2 us: per_device(): pl.pallas_call(kernel, out_shape=(jax.ShapeDtypeStruct((2, GROUP, KW_A, B...]
where the time goes in v1:
time: 73.4 us; the launch traced here: 73.3 us
  Pallas kernels  72.6 us (99%)
    pallas_call x1, Pallas kernels, per_device(): pl.pallas_call(kernel, out_shape=(jax.ShapeDtypeStruct((2, GROUP, KW_A, B...  63.2 us
    pallas_call x1, Pallas kernels, per_device(): pl.pallas_call(interpolate, out_shape=(jax.ShapeDtypeStruct((DAYS, CELLS)...  9.39 us

profile of v1, /device:TPU:1, one launch (start us, length us, event | category | flops | bytes accessed | tf_op | source)
XLA Modules:
  0.0 73.3 jit_solution(8865176812529567426)
XLA Ops:
  0.6 63.2 %shard_map.95 = (bf16[2,32,192,128]{3,2,1,0:T(8,128)(2,1)S(1)}, bf16[2,32,176,128]{3,2,1,0:T(8,128)(2,1)S(1)}, bf16[4096,2048]{1,0:T(8,128)(2,1)S(1)}, f32[72,4096]{1,0:T(8,128)S(1)}, s32[4,16]{1,0:T(4,128)S(1)}) custom-call(s32[1,4]{1,0:T(1,128)} %cond_hbm.1, s32[4,16]{1,0:T(4,128)} %tiles_hbm.1, bf16[1,366,128]{2,1,0:T(8,128)(2,1)} %bitcast.2, ...), custom_call_target="tpu_custom_call" | custom-call | tf_op jit(solution)/shard_map/pallas_call | solution.py:556
  63.9 9.4 %shard_map.96 = (bf16[366,4096]{1,0:T(8,128)(2,1)}, f32[4096]{0:T(1024)}) custom-call(bf16[2,32,192,128]{3,2,1,0:T(8,128)(2,1)S(1)} %get-tuple-element.9.kwa, bf16[2,32,176,128]{3,2,1,0:T(8,128)(2,1)S(1)} %get-tuple-element.10.kwb, bf16[4096,2048]{1,0:T(8,128)(2,1)S(1)} %get-tuple-element.11.cov, f32[72,4096]{1,0:T(8,128)S(1)} %get-tuple-element.12.rain_win, ...), custom_call_target="tpu_custom_call" | custom-call | tf_op jit(solution)/shard_map/pallas_call | solution.py:591
